TPU v7x, 32 devices: a whole 2x2x4 slice. The times are simulated.
32 devices in a mesh: groups: 2 (over y), seq: 4 (over z), tensor: 4 (over x, core).
Axes of the slice: x: 2, y: 2, z: 4, core: 2. Of those that a mesh axis runs over, the one named last changes fastest.
Arguments:
- text_states: bfloat16 [64, 8192], P(('groups', 'seq')), parts along dimension 0, may hold values from -18 to 18
- vision_states: bfloat16 [2048, 8192], P(('groups', 'seq'), 'tensor'), parts along dimension 0, may hold values from -6 to 6
- norm_gain: bfloat16 [8192], replicated, may hold values from 0.25 to 1.75
- query_weight: bfloat16 [8192, 8192], P('seq', 'tensor'), may hold values from -0.0625 to 0.0625
- key_value_weight: bfloat16 [2, 8192, 1024], P(None, 'tensor', 'seq'), may hold values from -0.0625 to 0.0625
- out_weight: bfloat16 [8192, 8192], P('tensor', 'seq'), may hold values from -0.0625 to 0.0625
- query_gain: float32 [128], replicated, may hold values from 4.5 to 6
- key_norm_gain: float32 [128], replicated, may hold values from 4.5 to 6
- attn_gate: float32 [1], replicated, may hold values from 0.4 to 2
- tile_counts: int32 [4], P('groups'), parts along dimension 0, may hold values from 128 to 512, as said below
- tile_mask: int32 [2, 2], P('groups'), parts along dimension 0, may hold values from 0 to 1, as said below
Outputs:
- layer_out: bfloat16 [64, 8192], P(('groups', 'tensor'), 'seq'), parts along dimension 0
There are 2 independent parts, one for each index of `groups`. A program takes and returns all parts, laid end to end along the dimension named above; an argument that names none is the same for every part. Nothing has to cross between parts.
Inputs may be any that keep to these rules, and one draw needn't show every extreme that they name: `tile_counts`: some tile is full (512 valid tokens) and some tile holds exactly 128; valid tokens are the first slots of a tile. `tile_mask`: every row has at least one 1 and at least one 0.
All inputs are finite; a program needn't handle non-finite values.
Results may differ from a plain program's by a relative error of at most 0.0055.
The roundings to bfloat16 on the way count: a program that leaves them out, or rounds other values in their place, can miss the bound.
Values may be sent and summed in bfloat16 or wider, within the bound.
A program may use at most 128 MiB of HBM per device.

v0:
```python
import jax
import jax.numpy as jnp
from jax import lax
from jax.sharding import PartitionSpec as P

TILE_LEN = 512
TEXT_BLOCK = 32
EPS = 1e-05
NEG = -1e30


def combined_all(part, axis, combine):
    gathered = jax.tree.map(lambda a: lax.all_gather(a, axis), part)

    def take(source):
        return jax.tree.map(lambda a: lax.dynamic_index_in_dim(a, source, 0, False), gathered)

    return lax.fori_loop(
        1, lax.axis_size(axis), lambda source, state: combine(state, take(source)), take(0)
    )


def root_mean_rows(value_matrix, gain):
    mean_sq = jnp.mean(value_matrix * value_matrix, axis=-1, keepdims=True)
    return value_matrix * lax.rsqrt(mean_sq + EPS) * gain


def allowed_mask(query_count, key_start, key_count, tile_counts, tile_mask):
    tiles = tile_counts.shape[0]
    blocks = tile_mask.shape[0]
    key_pos = key_start + jnp.arange(key_count, dtype=jnp.int32)
    key_tile = key_pos // TILE_LEN
    tile_match = key_tile[:, None] == jnp.arange(tiles, dtype=jnp.int32)[None, :]
    count_here = jnp.sum(jnp.where(tile_match, tile_counts[None, :], 0), axis=1)
    slot_ok = key_pos % TILE_LEN < count_here
    query_pos = jnp.arange(query_count, dtype=jnp.int32)
    block_match = (
        query_pos[:, None] // TEXT_BLOCK == jnp.arange(blocks, dtype=jnp.int32)[None, :]
    ).astype(jnp.float32)
    row_tiles = jnp.dot(block_match, tile_mask.astype(jnp.float32), precision=lax.Precision.HIGHEST)
    seen = jnp.dot(row_tiles, tile_match.astype(jnp.float32).T, precision=lax.Precision.HIGHEST)
    return (seen > 0.5) & slot_ok[None, :]


def partial_attend(query_matrix, key_matrix, value_matrix, allowed):
    scale = query_matrix.shape[-1] ** (-0.5)
    scores = (
        jnp.einsum("ihgd,khd->ihgk", query_matrix, key_matrix, preferred_element_type=jnp.float32)
        * scale
    )
    mask = allowed[:, None, None, :]
    masked = jnp.where(mask, scores, NEG)
    top = jnp.max(masked, axis=-1)
    weights = jnp.where(mask, jnp.exp(masked - top[..., None]), 0.0)
    total = jnp.sum(weights, axis=-1)
    summed = jnp.einsum("ihgk,khd->ihgd", weights, value_matrix, precision=lax.Precision.HIGHEST)
    return (top, total, summed)


def join_parts(first, second):
    top = jnp.maximum(first[0], second[0])
    scale_first = jnp.exp(first[0] - top)
    scale_second = jnp.exp(second[0] - top)
    total = first[1] * scale_first + second[1] * scale_second
    summed = first[2] * scale_first[..., None] + second[2] * scale_second[..., None]
    return (top, total, summed)


def local(
    text_states,
    vision_states,
    norm_gain,
    query_weight,
    key_value_weight,
    out_weight,
    query_gain,
    key_norm_gain,
    attn_gate,
    tile_counts,
    tile_mask,
):
    seq_count = lax.axis_size("seq")
    seq_index = lax.axis_index("seq")
    tensor_count = lax.axis_size("tensor")
    tensor_index = lax.axis_index("tensor")
    text_dev = text_states.shape[0]
    text_all = text_dev * seq_count
    vis_dev = vision_states.shape[0]
    head_size = query_gain.shape[0]
    query_local = query_weight.shape[1] // head_size
    normed = root_mean_rows(text_states.astype(jnp.float32), norm_gain.astype(jnp.float32)).astype(
        jnp.bfloat16
    )
    raw_cols, normed_cols = (
        lax.all_to_all(text_states, "seq", split_axis=1, concat_axis=0, tiled=True),
        lax.all_to_all(normed, "seq", split_axis=1, concat_axis=0, tiled=True),
    )
    rows = normed_cols
    query_raw = lax.psum_scatter(
        jnp.dot(rows, query_weight, preferred_element_type=jnp.float32),
        "seq",
        scatter_dimension=0,
        tiled=True,
    )
    query_matrix = root_mean_rows(
        query_raw.reshape(text_dev, query_local, head_size), query_gain
    ).astype(jnp.bfloat16)
    kv_full = jnp.einsum(
        "vd,jdc->jvc",
        vision_states,
        lax.all_gather(key_value_weight, "seq", axis=2, tiled=True),
        preferred_element_type=jnp.float32,
    )
    kv_local = lax.psum_scatter(kv_full, "tensor", scatter_dimension=2, tiled=True)
    kv_heads = kv_local.shape[2] // head_size
    group_size = query_local // kv_heads
    key_matrix = root_mean_rows(
        kv_local[0].reshape(vis_dev, kv_heads, head_size), key_norm_gain
    ).astype(jnp.bfloat16)
    value_matrix = kv_local[1].astype(jnp.bfloat16).reshape(vis_dev, kv_heads, head_size)
    queries_grouped = query_matrix.reshape(text_dev, kv_heads, group_size, head_size)
    query_all = lax.all_gather(queries_grouped, "seq", axis=0, tiled=True)
    allowed = allowed_mask(text_all, seq_index * vis_dev, vis_dev, tile_counts, tile_mask)
    local_parts = partial_attend(query_all, key_matrix, value_matrix.astype(jnp.float32), allowed)
    top, total, summed = combined_all(local_parts, "seq", join_parts)
    attention_all = (
        (summed / total[..., None]).reshape(text_all, query_local * head_size).astype(jnp.bfloat16)
    )
    rows_out = text_all // tensor_count
    rows = attention_all
    branch = lax.psum_scatter(
        jnp.dot(rows, out_weight, preferred_element_type=jnp.float32),
        "tensor",
        scatter_dimension=0,
        tiled=True,
    )
    residual = lax.dynamic_slice_in_dim(raw_cols, tensor_index * rows_out, rows_out, 0)
    return (residual.astype(jnp.float32) + jnp.tanh(attn_gate[0]) * branch).astype(jnp.bfloat16)


def solution(mesh):
    return jax.shard_map(
        local,
        mesh=mesh,
        in_specs=(
            P(("groups", "seq"), None),
            P(("groups", "seq"), "tensor"),
            P(),
            P("seq", "tensor"),
            P(None, "tensor", "seq"),
            P("tensor", "seq"),
            P(),
            P(),
            P(),
            P("groups"),
            P("groups", None),
        ),
        out_specs=P(("groups", "tensor"), "seq"),
        check_vma=False,
    )
```

profile of v0, /device:TPU:0, one launch (start us, length us, event | category | flops | bytes accessed | tf_op | source)
XLA Modules:
  0.0 289.4 jit_solution(2777696798040319785)
XLA Ops:
  6.5 4.1 %copy.87 = bf16[2,2048,256]{1,2,0:T(8,128)(2,1)} copy(bf16[2,2048,256]{2,1,0:T(8,128)(2,1)} %param.17) | data formatting | bytes 4194304 | tf_op args[4]
  10.7 0.7 convert_element_type.43
  11.4 1.1 fusion.9
  12.5 1.0 fusion.11
  13.5 12.2 %all_to_all.38 = bf16[8,4,2048]{2,0,1:T(8,128)(2,1)S(1)} all-to-all(bf16[8,4,2048]{2,0,1:T(8,128)(2,1)S(1)} %bitcast.84), channel_id=1, replica_groups=mesh['groups'=2,'seq'=4,'tensor'=4] {'seq'}, dimensions={1} | all-to-all | bytes 262144 | tf_op jit(solution)/shard_map/all_to_all | solution.py:96
  25.7 5.9 %fusion.20 = f32[32,2048]{1,0:T(8,128)} fusion(bf16[2048,2048]{1,0:T(8,128)(2,1)} %param.16, bf16[8,4,2048]{2,0,1:T(8,128)(2,1)S(1)} %all_to_all.38), kind=kOutput, calls=%fused_computation.36 | convolution fusion | flops 268435456 | bytes 8781824 | tf_op jit(solution)/shard_map/dot_general | solution.py:100
  31.8 131.4 %all-gather.6.cloned.1.call-done = bf16[2,2048,1024]{1,2,0:T(8,128)(2,1)} async-done(((bf16[2,2048,256]{1,2,0:T(8,128)(2,1)}), bf16[2,2048,1024]{1,2,0:T(8,128)(2,1)}) %all-gather.6.cloned.1.call-update) | async-done | bytes 8388624 | tf_op jit(solution)/shard_map/all_gather | solution.py:111
  163.2 7.2 %convolution_bitcast_fusion = f32[2,256,1024]{1,2,0:T(8,128)} fusion(bf16[2,2048,1024]{1,2,0:T(8,128)(2,1)} %all-gather.6.cloned.1.call-done, bf16[256,2048]{1,0:T(8,128)(2,1)S(1)} %copy-done), kind=kOutput, calls=%fused_computation.10 | convolution fusion | flops 2147483648 | bytes 11534336 | tf_op jit(solution)/shard_map/vd,jdc->jvc/dot_general | solution.py:108
  170.8 12.5 %reduce-scatter.6.cloned.1.call-done = f32[8,2048]{1,0:T(8,128)} async-done(((f32[32,2048]{1,0:T(8,128)}), f32[8,2048]{1,0:T(8,128)}) %reduce-scatter.6.cloned.1.call-update) | async-done | bytes 65552 | tf_op jit(solution)/shard_map/reduce_scatter | solution.py:99
  183.3 0.9 bitcast_reduce_fusion
  184.4 0.9 multiply_convert_fusion.1
  185.3 12.3 %all_gather.25 = bf16[32,2,8,128]{3,0,2,1:T(8,128)(2,1)S(1)} all-gather(bf16[8,2,8,128]{3,0,2,1:T(8,128)(2,1)S(1)} %multiply_convert_fusion.1), channel_id=1, replica_groups=mesh['groups'=2,'seq'=4,'tensor'=4] {'seq'}, dimensions={0}, use_global_device_ids=true | all-gather | bytes 163840 | tf_op jit(solution)/shard_map/all_gather | solution.py:122
  197.6 18.1 %reduce-scatter.4.cloned.1.call-done = f32[2,256,256]{1,2,0:T(8,128)} async-done(((f32[2,256,1024]{1,2,0:T(8,128)}), f32[2,256,256]{1,2,0:T(8,128)}) %reduce-scatter.4.cloned.1.call-update) | async-done | bytes 524304 | tf_op jit(solution)/shard_map/reduce_scatter | solution.py:114
  215.7 1.0 slice.15
  216.8 0.4 fusion.33
  217.2 1.0 slice.21
  218.2 1.2 convolution_bitcast_fusion.1
  219.9 13.8 %all-gather.1 = f32[128,2,8]{2,1,0:T(2,128)S(1)} all-gather(f32[32,2,8]{2,1,0:T(2,128)S(1)} %copy.92), channel_id=3, replica_groups=mesh['groups'=2,'seq'=4,'tensor'=4] {'seq'}, dimensions={0}, use_global_device_ids=true | all-gather | bytes 10240 | tf_op jit(solution)/shard_map/all_gather | solution.py:13
  233.9 14.5 %all-gather = f32[128,2,8]{2,1,0:T(2,128)S(1)} all-gather(f32[32,2,8]{2,1,0:T(2,128)S(1)} %copy.91), channel_id=2, replica_groups=mesh['groups'=2,'seq'=4,'tensor'=4] {'seq'}, dimensions={0}, use_global_device_ids=true | all-gather | bytes 10240 | tf_op jit(solution)/shard_map/all_gather | solution.py:13
  248.5 2.2 all-gather.8.cloned.1.call-done
  250.7 1.0 slice.19
  251.9 4.5 %while.19 = (s32[]{:T(128)}, f32[32,2,8]{0,2,1:T(8,128)S(1)}, f32[32,2,8]{0,2,1:T(8,128)S(1)}, f32[32,2,8,128]{3,2,1,0:T(8,128)S(1)}, f32[4,32,2,8]{1,3,2,0:T(8,...) while((s32[]{:T(128)}, f32[32,2,8]{0,2,1:T(8,128)S(1)}, ...), condition=%wide.region_9.10_spmd, body=%wide.region_8.9_spmd.sunk | while | flops 199685 | bytes 1339543 | solution.py:18
  252.1 1.0 constant_dynamic-slice_fusion.2
  253.1 0.3 fusion.42
  253.6 1.0 constant_dynamic-slice_fusion.2
  254.6 0.3 fusion.42
  255.1 1.0 constant_dynamic-slice_fusion.2
  256.6 5.6 %fusion.17 = f32[32,2048]{1,0:T(8,128)} fusion(bf16[2048,2048]{1,0:T(8,128)(2,1)} %param.18, bf16[4,8,16,128]{3,2,1,0:T(8,128)(2,1)S(1)} %bitcast.80), kind=kOutput, calls=%fused_computation.33 | convolution fusion | flops 268435456 | bytes 8781824 | tf_op jit(solution)/shard_map/dot_general | solution.py:132
  262.3 3.3 %all-to-all-start = ((bf16[8,4,2048]{2,0,1:T(8,128)(2,1)}), bf16[8,4,2048]{2,0,1:T(8,128)(2,1)S(1)}, u32[]{:S(2)}, u32[]{:S(2)}) async-start(bf16[8,4,2048]{2,0,1:T(8,128)(2,1)} %bitcast.3), calls=%async_computation | async-start | bytes 262144 | tf_op jit(solution)/shard_map/all_to_all | solution.py:95
  266.3 5.5 %all-to-all-done = bf16[8,4,2048]{2,0,1:T(8,128)(2,1)S(1)} async-done(((bf16[8,4,2048]{2,0,1:T(8,128)(2,1)}), bf16[8,4,2048]{2,0,1:T(8,128)(2,1)S(1)}, u32[]{:S(2)}, u32[]{:S(2)}) %all-to-all-start) | async-done | bytes 131104 | tf_op jit(solution)/shard_map/all_to_all | solution.py:95
  271.9 9.6 %reduce-scatter.8.cloned.1.call-done = f32[8,2048]{1,0:T(8,128)} async-done(((f32[32,2048]{1,0:T(8,128)}), f32[8,2048]{1,0:T(8,128)}) %reduce-scatter.8.cloned.1.call-update) | async-done | bytes 65552 | tf_op jit(solution)/shard_map/reduce_scatter | solution.py:131
  281.4 1.5 add_convert_fusion
  (55 shorter events, 3.0 us)
Async XLA Ops:
  6.5 156.6 %copy-start = (bf16[256,2048]{1,0:T(8,128)(2,1)S(1)}, bf16[256,2048]{1,0:T(8,128)(2,1)}, u32[]{:S(2)}) copy-start(bf16[256,2048]{1,0:T(8,128)(2,1)} %param.14) | copy-start | bytes 3145732
  6.5 156.6 %all-gather.6.cloned.1.call-start = ((), (), s32[]{:S(2)}) async-start(), calls=%async_computation.5 | async-start | bytes 10485760 | tf_op jit(solution)/shard_map/all_gather | solution.py:111
  10.7 172.6 %reduce-scatter.6.cloned.1.call-start = ((), (), s32[]{:S(2)}) async-start(), calls=%async_computation.7 | async-start | bytes 327680 | tf_op jit(solution)/shard_map/reduce_scatter | solution.py:99
  31.7 138.8 %copy-start.3 = (s32[2]{0:T(128)S(1)}, s32[2]{0:T(128)}, u32[]{:S(2)}) copy-start(s32[2]{0:T(128)} %param.22) | copy-start | bytes 28
  31.7 138.9 %copy-start.4 = (s32[1,2]{1,0:T(1,128)S(1)}, s32[1,2]{1,0:T(1,128)}, u32[]{:S(2)}) copy-start(s32[1,2]{1,0:T(1,128)} %param.23) | copy-start | bytes 28
  31.7 152.7 %copy-start.1 = (f32[128]{0:T(128)S(1)}, f32[128]{0:T(128)}, u32[]{:S(2)}) copy-start(f32[128]{0:T(128)} %param.19) | copy-start | bytes 1540
  31.7 185.1 %copy-start.2 = (f32[128]{0:T(128)S(1)}, f32[128]{0:T(128)}, u32[]{:S(2)}) copy-start(f32[128]{0:T(128)} %param.20) | copy-start | bytes 1540
  31.7 184.0 %reduce-scatter.4.cloned.1.call-start = ((), (), s32[]{:S(2)}) async-start(), calls=%async_computation.6 | async-start | bytes 2621440 | tf_op jit(solution)/shard_map/reduce_scatter | solution.py:114
  170.3 80.4 %all-gather.8.cloned.1.call-start = ((), (), s32[]{:S(2)}) async-start(), calls=%async_computation.9 | async-start | bytes 1310720 | tf_op jit(solution)/shard_map/all_gather | solution.py:13
  219.4 62.0 %reduce-scatter.8.cloned.1.call-start = ((), (), s32[]{:S(2)}) async-start(), calls=%async_computation.8 | async-start | bytes 327680 | tf_op jit(solution)/shard_map/reduce_scatter | solution.py:131
  262.3 9.6 %all-to-all-start = ((bf16[8,4,2048]{2,0,1:T(8,128)(2,1)}), bf16[8,4,2048]{2,0,1:T(8,128)(2,1)S(1)}, u32[]{:S(2)}, u32[]{:S(2)}) async-start(bf16[8,4,2048]{2,0,1:T(8,128)(2,1)} %bitcast.3), calls=%async_computation | async-start | bytes 262144 | tf_op jit(solution)/shard_map/all_to_all | solution.py:95
Sparse Core Ops, SparseCore 0:
  10.8 152.3 all-gather.5
  165.4 17.8 reduce-scatter.5
  186.0 29.6 reduce-scatter.3
  219.6 31.1 all-gather.7
  262.4 18.9 reduce-scatter.7
where the time goes:
time: 290 us; the launch traced here: 289 us
  waiting for transfers between devices  179 us (62%)
  blocking collectives  52.7 us (18%)
  matrix products  20.5 us (7%)
  between operations  14 us (5%)
  local copies, waits for them, and re-layouts  11.5 us (4%)
  other arithmetic  7.69 us (3%)
  starting transfers between devices  3.51 us (1%)
    all_gather x1, waiting for transfers between devices, local(): lax.all_gather(key_value_weight, 'seq', axis=2, tiled=True)  131 us
    all_gather x2, blocking collectives, combined_all(): gathered = jax.tree.map(lambda a: lax.all_gather(a, axis), part)  28.2 us
    reduce_scatter x1, waiting for transfers between devices, local(): lax.psum_scatter(kv_full, 'tensor', scatter_dimension=2, tiled=True)  18.1 us
    reduce_scatter x1, waiting for transfers between devices, local(): lax.psum_scatter(jnp.dot(rows, query_weight, preferred_element_type=jnp.f...  12.5 us
    all_gather x1, blocking collectives, local(): query_all = lax.all_gather(queries_grouped, 'seq', axis=0, tiled=True)  12.3 us
    all_to_all x1, blocking collectives, local(): lax.all_to_all(normed, 'seq', split_axis=1, concat_axis=0, tiled=True)  12.2 us
    reduce_scatter x1, waiting for transfers between devices, local(): lax.psum_scatter(jnp.dot(rows, out_weight, preferred_element_type=jnp.flo...  9.56 us
    dot_general x1, matrix products, local(): jnp.einsum('vd,jdc->jvc', vision_states, lax.all_gather(key_value_weight,...  7.17 us
  transfers between devices with their start and end apart: 6, of which 6 were waited for; matrix products, arithmetic and copies ran while one was open for 7% of the time, Pallas kernels for 0%

commit v1 on v0

--- a/solution.py
+++ b/solution.py
@@ -7,6 +7,22 @@
 TEXT_BLOCK = 32
 EPS = 1e-05
 NEG = -1e30
+
+
+def collect(x, axis, dim):
+    ways, here, step = (lax.axis_size(axis), lax.axis_index(axis), x.shape[dim])
+    shape = [n * ways if d == dim else n for d, n in enumerate(x.shape)]
+    full = lax.dynamic_update_slice_in_dim(jnp.zeros(shape, x.dtype), x, here * step, axis=dim)
+    going_up = going_down = x
+    for far in range(1, ways // 2 + 1):
+        going_up = lax.ppermute(going_up, axis, [(d, (d + 1) % ways) for d in range(ways)])
+        full = lax.dynamic_update_slice_in_dim(full, going_up, (here - far) % ways * step, axis=dim)
+        if 2 * far < ways:
+            going_down = lax.ppermute(going_down, axis, [(d, (d - 1) % ways) for d in range(ways)])
+            full = lax.dynamic_update_slice_in_dim(
+                full, going_down, (here + far) % ways * step, axis=dim
+            )
+    return full
 
 
 def combined_all(part, axis, combine):
@@ -108,7 +124,7 @@
     kv_full = jnp.einsum(
         "vd,jdc->jvc",
         vision_states,
-        lax.all_gather(key_value_weight, "seq", axis=2, tiled=True),
+        collect(key_value_weight, "seq", 2),
         preferred_element_type=jnp.float32,
     )
     kv_local = lax.psum_scatter(kv_full, "tensor", scatter_dimension=2, tiled=True)

time: 290 us -> 285 us (0.983)
  waiting for transfers between devices: 179 us -> 113 us
  starting transfers between devices: 3.51 us -> 55.2 us
  local copies, waits for them, and re-layouts: 11.5 us -> 31.9 us
  blocking collectives: 52.7 us -> 40.5 us
    all_gather x1 -> x0, waiting for transfers between devices: 131 us -> none  [local(): lax.all_gather(key_value_weight, 'seq', axis=2, tiled=True)]
    all_to_all x0 -> x1, starting transfers between devices: none -> 46.7 us  [local(): lax.all_to_all(normed, 'seq', split_axis=1, concat_axis=0, tiled=True)]
    ppermute x0 -> x3, waiting for transfers between devices: none -> 45 us  [the longest x2 45 us: collect(): lax.ppermute(going_up, axis, [(d, (d + 1) % ways) for d in range(ways)])]
    all_to_all x0 -> x1, waiting for transfers between devices: none -> 34.7 us  [local(): lax.all_to_all(normed, 'seq', split_axis=1, concat_axis=0, tiled=True)]
    reduce_scatter x1, waiting for transfers between devices: 12.5 us -> 0.02 us  [local(): lax.psum_scatter(jnp.dot(rows, query_weight, preferred_element_type=jnp.f...]
    all_to_all x1 -> x0, blocking collectives: 12.2 us -> none  [local(): lax.all_to_all(normed, 'seq', split_axis=1, concat_axis=0, tiled=True)]
    ppermute x0 -> x3, local copies, waits for them, and re-layouts: none -> 9.87 us  [the longest x2 5.88 us: collect(): lax.ppermute(going_up, axis, [(d, (d + 1) % ways) for d in range(ways)])]
    dynamic_update_slice x0 -> x4, local copies, waits for them, and re-layouts: none -> 7.48 us  [the longest x1 3.16 us: collect(): lax.dynamic_update_slice_in_dim(full, going_down, (here + far) % ways * s...]
  transfers between devices with their start and end apart: 6 -> 9, of which waited for: 6 -> 6; matrix products, arithmetic and copies ran while one was open for 7% -> 16% of each run, Pallas kernels for 0% -> 0%
where the time goes in v1:
time: 285 us; the launch traced here: 284 us
  waiting for transfers between devices  113 us (40%)
  starting transfers between devices  55.2 us (19%)
  blocking collectives  40.5 us (14%)
  local copies, waits for them, and re-layouts  31.9 us (11%)
  matrix products  20.3 us (7%)
  between operations  14.1 us (5%)
  other arithmetic  8.33 us (3%)
    all_to_all x1, starting transfers between devices, local(): lax.all_to_all(normed, 'seq', split_axis=1, concat_axis=0, tiled=True)  46.7 us
    ppermute x2, waiting for transfers between devices, collect(): lax.ppermute(going_up, axis, [(d, (d + 1) % ways) for d in range(ways)])  45 us
    all_to_all x1, waiting for transfers between devices, local(): lax.all_to_all(normed, 'seq', split_axis=1, concat_axis=0, tiled=True)  34.7 us
    all_gather x2, blocking collectives, combined_all(): gathered = jax.tree.map(lambda a: lax.all_gather(a, axis), part)  28.2 us
    reduce_scatter x1, waiting for transfers between devices, local(): lax.psum_scatter(kv_full, 'tensor', scatter_dimension=2, tiled=True)  16.1 us
    all_gather x1, blocking collectives, local(): query_all = lax.all_gather(queries_grouped, 'seq', axis=0, tiled=True)  12.3 us
    reduce_scatter x1, waiting for transfers between devices, local(): lax.psum_scatter(jnp.dot(rows, out_weight, preferred_element_type=jnp.flo...  9.52 us
    dot_general x1, matrix products, local(): jnp.einsum('vd,jdc->jvc', vision_states, collect(key_value_weight, 'seq',...  7.24 us
  transfers between devices with their start and end apart: 9, of which 6 were waited for; matrix products, arithmetic and copies ran while one was open for 16% of the time, Pallas kernels for 0%

profile of v1, /device:TPU:0, one launch (start us, length us, event | category | flops | bytes accessed | tf_op | source)
XLA Modules:
  0.0 283.6 jit_solution(15184674129778385231)
XLA Ops:
  6.5 3.0 %collective-permute-start = (bf16[2,2048,256]{2,1,0:T(8,128)(2,1)}, bf16[2,2048,256]{2,1,0:T(8,128)(2,1)}, u32[]{:S(2)}, u32[]{:S(2)}) collective-permute-start(bf16[2,2048,256]{2,1,0:T(8,128)(2,1)} %param.17), channel_id=1, source_target_pairs={{0,4},{4,8},{8,12},{12,0},{1,5},{5,9},{9,13},{13,1},{2,6},{6,10},{... | collective-permute-start | bytes 6291464 | tf_op jit(solution)/shard_map/ppermute | solution.py:18
  9.6 2.0 collective-permute-start.1
  12.3 1.1 fusion.9
  13.4 45.0 %collective-permute-done = bf16[2,2048,256]{2,1,0:T(8,128)(2,1)} collective-permute-done((bf16[2,2048,256]{2,1,0:T(8,128)(2,1)}, bf16[2,2048,256]{2,1,0:T(8,128)(2,1)}, u32[]{:S(2)}, u32[]{:S(2)}) %collective-permute-start) | collective-permute-done | bytes 2097184 | tf_op jit(solution)/shard_map/ppermute | solution.py:18
  58.4 1.6 fusion.11
  60.1 46.7 %all-to-all-start.1 = ((bf16[8,4,2048]{2,0,1:T(8,128)(2,1)}), bf16[8,4,2048]{2,0,1:T(8,128)(2,1)S(1)}, u32[]{:S(2)}, u32[]{:S(2)}) async-start(bf16[8,4,2048]{2,0,1:T(8,128)(2,1)} %bitcast.14), calls=%async_computation.2 | async-start | bytes 262144 | tf_op jit(solution)/shard_map/all_to_all | solution.py:112
  106.7 2.9 %copy.102 = bf16[2,2048,256]{1,2,0:T(8,128)(2,1)S(1)} copy(bf16[2,2048,256]{2,1,0:T(8,128)(2,1)} %param.17) | data formatting | bytes 4194304 | tf_op args[4]
  109.7 4.3 %broadcast_in_dim.56 = bf16[2,2048,1024]{1,2,0:T(8,128)(2,1)} broadcast(bf16[]{:T(256)} %constant.146.clone.1), dimensions={} | broadcast | bytes 8388610 | tf_op jit(solution)/shard_map/broadcast_in_dim | solution.py:15
  114.0 1.4 constant_dynamic-update-slice_fusion.3
  115.4 34.7 %all-to-all-done.1 = bf16[8,4,2048]{2,0,1:T(8,128)(2,1)S(1)} async-done(((bf16[8,4,2048]{2,0,1:T(8,128)(2,1)}), bf16[8,4,2048]{2,0,1:T(8,128)(2,1)S(1)}, u32[]{:S(2)}, u32[]{:S(2)}) %all-to-all-start.1) | async-done | bytes 131104 | tf_op jit(solution)/shard_map/all_to_all | solution.py:112
  150.1 5.6 %fusion.20 = f32[32,2048]{1,0:T(8,128)} fusion(bf16[2048,2048]{1,0:T(8,128)(2,1)} %param.16, bf16[8,4,2048]{2,0,1:T(8,128)(2,1)S(1)} %all-to-all-done.1), kind=kOutput, calls=%fused_computation.36 | convolution fusion | flops 268435456 | bytes 8781824 | tf_op jit(solution)/shard_map/dot_general | solution.py:116
  155.8 2.9 %copy.103 = bf16[2,2048,256]{1,2,0:T(8,128)(2,1)S(1)} copy(bf16[2,2048,256]{2,1,0:T(8,128)(2,1)} %collective-permute-done) | data formatting | bytes 4194304 | tf_op jit(solution)/shard_map/ppermute | solution.py:18
  158.8 4.0 %copy.104 = bf16[2,2048,256]{1,2,0:T(8,128)(2,1)} copy(bf16[2,2048,256]{2,1,0:T(8,128)(2,1)} %collective-permute-done.1) | data formatting | bytes 4194304 | tf_op jit(solution)/shard_map/ppermute | solution.py:21
  162.8 1.4 constant_dynamic-update-slice_fusion.2
  164.2 3.2 %constant_dynamic-update-slice_fusion.1 = bf16[2,2048,1024]{1,2,0:T(8,128)(2,1)} fusion(bf16[2,2048,1024]{1,2,0:T(8,128)(2,1)} %constant_dynamic-update-slice_fusion.2, bf16[2,2048,256]{1,2,0:T(8,128)(2,1)} %copy.104, s32[]{:T(128)S(6)} %select_n.107), kind=kLoop, calls=%fused_computation.58 | loop fusion | bytes 4194308 | tf_op jit(solution)/shard_map/dynamic_update_slice | solution.py:22
  167.4 2.9 %copy.105 = bf16[2,2048,256]{1,2,0:T(8,128)(2,1)S(1)} copy(bf16[2,2048,256]{2,1,0:T(8,128)(2,1)} %collective-permute-done.2) | data formatting | bytes 4194304 | tf_op jit(solution)/shard_map/ppermute | solution.py:18
  170.3 1.5 constant_dynamic-update-slice_fusion
  171.8 7.2 %convolution_bitcast_fusion = f32[2,256,1024]{1,2,0:T(8,128)} fusion(bf16[2,2048,1024]{1,2,0:T(8,128)(2,1)} %constant_dynamic-update-slice_fusion, bf16[256,2048]{1,0:T(8,128)(2,1)S(1)} %copy-done), kind=kOutput, calls=%fused_computation.10 | convolution fusion | flops 2147483648 | bytes 11534336 | tf_op jit(solution)/shard_map/vd,jdc->jvc/dot_general | solution.py:124
  181.5 12.3 %all_gather.21 = bf16[32,2,8,128]{3,0,2,1:T(8,128)(2,1)S(1)} all-gather(bf16[8,2,8,128]{3,0,2,1:T(8,128)(2,1)S(1)} %multiply_convert_fusion.1), channel_id=1, replica_groups=mesh['groups'=2,'seq'=4,'tensor'=4] {'seq'}, dimensions={0}, use_global_device_ids=true | all-gather | bytes 163840 | tf_op jit(solution)/shard_map/all_gather | solution.py:138
  193.8 16.1 %reduce-scatter.4.cloned.1.call-done = f32[2,256,256]{1,2,0:T(8,128)} async-done(((f32[2,256,1024]{1,2,0:T(8,128)}), f32[2,256,256]{1,2,0:T(8,128)}) %reduce-scatter.4.cloned.1.call-update) | async-done | bytes 524304 | tf_op jit(solution)/shard_map/reduce_scatter | solution.py:130
  212.5 1.2 convolution_bitcast_fusion.1
  214.2 13.8 %all-gather.1 = f32[128,2,8]{2,1,0:T(2,128)S(1)} all-gather(f32[32,2,8]{2,1,0:T(2,128)S(1)} %copy.110), channel_id=3, replica_groups=mesh['groups'=2,'seq'=4,'tensor'=4] {'seq'}, dimensions={0}, use_global_device_ids=true | all-gather | bytes 10240 | tf_op jit(solution)/shard_map/all_gather | solution.py:29
  228.1 14.5 %all-gather = f32[128,2,8]{2,1,0:T(2,128)S(1)} all-gather(f32[32,2,8]{2,1,0:T(2,128)S(1)} %copy.109), channel_id=2, replica_groups=mesh['groups'=2,'seq'=4,'tensor'=4] {'seq'}, dimensions={0}, use_global_device_ids=true | all-gather | bytes 10240 | tf_op jit(solution)/shard_map/all_gather | solution.py:29
  242.7 2.2 all-gather.5.cloned.1.call-done
  246.1 4.5 %while.19 = (s32[]{:T(128)}, f32[32,2,8]{0,2,1:T(8,128)S(1)}, f32[32,2,8]{0,2,1:T(8,128)S(1)}, f32[32,2,8,128]{3,2,1,0:T(8,128)S(1)}, f32[4,32,2,8]{1,3,2,0:T(8,...) while((s32[]{:T(128)}, f32[32,2,8]{0,2,1:T(8,128)S(1)}, ...), condition=%wide.region_9.10_spmd, body=%wide.region_8.9_spmd.sunk | while | flops 199685 | bytes 1339543 | solution.py:34
  246.3 1.0 constant_dynamic-slice_fusion.2
  247.8 1.0 constant_dynamic-slice_fusion.2
  250.9 5.6 %fusion.17 = f32[32,2048]{1,0:T(8,128)} fusion(bf16[2048,2048]{1,0:T(8,128)(2,1)} %param.18, bf16[4,8,16,128]{3,2,1,0:T(8,128)(2,1)S(1)} %bitcast.80), kind=kOutput, calls=%fused_computation.33 | convolution fusion | flops 268435456 | bytes 8781824 | tf_op jit(solution)/shard_map/dot_general | solution.py:148
  256.5 3.3 %all-to-all-start = ((bf16[8,4,2048]{2,0,1:T(8,128)(2,1)}), bf16[8,4,2048]{2,0,1:T(8,128)(2,1)S(1)}, u32[]{:S(2)}, u32[]{:S(2)}) async-start(bf16[8,4,2048]{2,0,1:T(8,128)(2,1)} %bitcast.3), calls=%async_computation | async-start | bytes 262144 | tf_op jit(solution)/shard_map/all_to_all | solution.py:111
  260.6 5.5 %all-to-all-done = bf16[8,4,2048]{2,0,1:T(8,128)(2,1)S(1)} async-done(((bf16[8,4,2048]{2,0,1:T(8,128)(2,1)}), bf16[8,4,2048]{2,0,1:T(8,128)(2,1)S(1)}, u32[]{:S(2)}, u32[]{:S(2)}) %all-to-all-start) | async-done | bytes 131104 | tf_op jit(solution)/shard_map/all_to_all | solution.py:111
  266.1 9.5 %reduce-scatter.8.cloned.1.call-done = f32[8,2048]{1,0:T(8,128)} async-done(((f32[32,2048]{1,0:T(8,128)}), f32[8,2048]{1,0:T(8,128)}) %reduce-scatter.8.cloned.1.call-update) | async-done | bytes 65552 | tf_op jit(solution)/shard_map/reduce_scatter | solution.py:147
  275.6 1.5 add_convert_fusion
  (67 shorter events, 10.4 us)
Async XLA Ops:
  6.5 165.3 %copy-start = (bf16[256,2048]{1,0:T(8,128)(2,1)S(1)}, bf16[256,2048]{1,0:T(8,128)(2,1)}, u32[]{:S(2)}) copy-start(bf16[256,2048]{1,0:T(8,128)(2,1)} %param.14) | copy-start | bytes 3145732
  6.5 51.9 %collective-permute-start = (bf16[2,2048,256]{2,1,0:T(8,128)(2,1)}, bf16[2,2048,256]{2,1,0:T(8,128)(2,1)}, u32[]{:S(2)}, u32[]{:S(2)}) collective-permute-start(bf16[2,2048,256]{2,1,0:T(8,128)(2,1)} %param.17), channel_id=1, source_target_pairs={{0,4},{4,8},{8,12},{12,0},{1,5},{5,9},{9,13},{13,1},{2,6},{6,10},{... | collective-permute-start | bytes 6291464 | tf_op jit(solution)/shard_map/ppermute | solution.py:18
  9.6 149.2 %collective-permute-start.1 = (bf16[2,2048,256]{2,1,0:T(8,128)(2,1)}, bf16[2,2048,256]{2,1,0:T(8,128)(2,1)}, u32[]{:S(2)}, u32[]{:S(2)}) collective-permute-start(bf16[2,2048,256]{2,1,0:T(8,128)(2,1)} %param.17), channel_id=1, source_target_pairs={{0,12},{4,0},{8,4},{12,8},{1,13},{5,1},{9,5},{13,9},{2,14},{6,2},{... | collective-permute-start | bytes 6291464 | tf_op jit(solution)/shard_map/ppermute | solution.py:21
  58.4 109.0 %collective-permute-start.2 = (bf16[2,2048,256]{2,1,0:T(8,128)(2,1)}, bf16[2,2048,256]{2,1,0:T(8,128)(2,1)}, u32[]{:S(2)}, u32[]{:S(2)}) collective-permute-start(bf16[2,2048,256]{2,1,0:T(8,128)(2,1)} %collective-permute-done), channel_id=1, source_target_pairs={{0,4},{4,8},{8,12},{12,0},{1,5},{5,9},{9,13},{13,1},{2,6},{6,10},{... | collective-permute-start | bytes 6291464 | tf_op jit(solution)/shard_map/ppermute | solution.py:18
  60.1 90.1 %all-to-all-start.1 = ((bf16[8,4,2048]{2,0,1:T(8,128)(2,1)}), bf16[8,4,2048]{2,0,1:T(8,128)(2,1)S(1)}, u32[]{:S(2)}, u32[]{:S(2)}) async-start(bf16[8,4,2048]{2,0,1:T(8,128)(2,1)} %bitcast.14), calls=%async_computation.2 | async-start | bytes 262144 | tf_op jit(solution)/shard_map/all_to_all | solution.py:112
  106.7 72.8 %reduce-scatter.6.cloned.1.call-start = ((), (), s32[]{:S(2)}) async-start(), calls=%async_computation.6 | async-start | bytes 327680 | tf_op jit(solution)/shard_map/reduce_scatter | solution.py:115
  155.8 54.1 %reduce-scatter.4.cloned.1.call-start = ((), (), s32[]{:S(2)}) async-start(), calls=%async_computation.5 | async-start | bytes 2621440 | tf_op jit(solution)/shard_map/reduce_scatter | solution.py:130
  171.8 7.4 %copy-start.3 = (s32[2]{0:T(128)S(1)}, s32[2]{0:T(128)}, u32[]{:S(2)}) copy-start(s32[2]{0:T(128)} %param.22) | copy-start | bytes 28
  171.8 7.5 %copy-start.4 = (s32[1,2]{1,0:T(1,128)S(1)}, s32[1,2]{1,0:T(1,128)}, u32[]{:S(2)}) copy-start(s32[1,2]{1,0:T(1,128)} %param.23) | copy-start | bytes 28
  171.8 8.8 %copy-start.1 = (f32[128]{0:T(128)S(1)}, f32[128]{0:T(128)}, u32[]{:S(2)}) copy-start(f32[128]{0:T(128)} %param.19) | copy-start | bytes 1540
  171.8 39.3 %copy-start.2 = (f32[128]{0:T(128)S(1)}, f32[128]{0:T(128)}, u32[]{:S(2)}) copy-start(f32[128]{0:T(128)} %param.20) | copy-start | bytes 1540
  179.1 65.9 %all-gather.5.cloned.1.call-start = ((), (), s32[]{:S(2)}) async-start(), calls=%async_computation.8 | async-start | bytes 1310720 | tf_op jit(solution)/shard_map/all_gather | solution.py:29
  213.7 61.9 %reduce-scatter.8.cloned.1.call-start = ((), (), s32[]{:S(2)}) async-start(), calls=%async_computation.7 | async-start | bytes 327680 | tf_op jit(solution)/shard_map/reduce_scatter | solution.py:147
  256.5 9.6 %all-to-all-start = ((bf16[8,4,2048]{2,0,1:T(8,128)(2,1)}), bf16[8,4,2048]{2,0,1:T(8,128)(2,1)S(1)}, u32[]{:S(2)}, u32[]{:S(2)}) async-start(bf16[8,4,2048]{2,0,1:T(8,128)(2,1)} %bitcast.3), calls=%async_computation | async-start | bytes 262144 | tf_op jit(solution)/shard_map/all_to_all | solution.py:111
Sparse Core Ops, SparseCore 0:
  155.9 18.9 reduce-scatter.5
  179.2 30.6 reduce-scatter.3
  213.8 31.1 all-gather.4
  256.6 18.9 reduce-scatter.7
